TPU v7x, 256 devices: a whole 4x4x8 slice. The times are simulated.
256 devices in a mesh: cluster: 8 (over z), view: 32 (over y, x, core).
Axes of the slice: x: 4, y: 4, z: 8, core: 2. Of those that a mesh axis runs over, the one named last changes fastest.
Arguments:
- latents: bfloat16 [8, 32, 128, 1024], P('cluster', 'view'), may hold values from -6 to 6
- gain: float32 [1024], replicated, may hold values from 0.1 to 1.9
- w_query: bfloat16 [1024, 1024], replicated, may hold values from -2 to 2
- w_key: bfloat16 [1024, 1024], replicated, may hold values from -2 to 2
- w_value: bfloat16 [1024, 1024], replicated, may hold values from -0.1875 to 0.1875
- w_out: bfloat16 [1024, 1024], replicated, may hold values from -0.1875 to 0.1875
- pair_list: int32 [512, 3], replicated, may hold values from 0 to 255, as said below
Outputs:
- attended: bfloat16 [8, 32, 128, 1024], P('cluster', 'view')
Inputs may be any that keep to these rules, and one draw needn't show every extreme that they name: `pair_list`: each row holds two different views, either in the same cluster at positions that differ by 1 to 3 (wrapping around the cluster), or at the same position in neighbouring clusters (wrapping); the third entry equals one of the two. No pair stands twice, in either order.
All inputs are finite; a program needn't handle non-finite values.
Results may differ from a plain program's by a relative error of at most 0.014.
Values may be sent and summed in bfloat16 or wider, within the bound.
A program may use at most 128 MiB of HBM per device.

v0:
```python
import functools
import jax
import jax.numpy as jnp
from jax import lax
from jax.experimental import pallas as pl
from jax.experimental.pallas import tpu as pltpu
from jax.sharding import PartitionSpec as P

MESH = pl.DeviceIdType.MESH
BF = jnp.bfloat16
F32 = jnp.float32
TOK, D, PAIR, NP = 128, 1024, 128, 8
GA, GB, GZ, GD, GE = range(5)
NONE = -1e30
COMM = True
SKIP = ""
SENDS = "abzZfs"
DEP = 2
DEPE = 2
LATEB = True
COPYK = False
XDOT = False
VL = 62 * 2**20
UN = 8


def dot(a, b):
    return jnp.dot(a, b, preferred_element_type=F32)


def kernel(lat_hbm, gain_hbm, wq_hbm, wk_hbm, wv_hbm, wo_hbm, pl_hbm, out_hbm,
           raw, gain, wq, wkv, wo, plist, own, xb, xz, xe, kbuf, vt, qt, acc, mx, tot, bias, mg, outv,
           lsem, wsem, osem, ssem, rsem, ack):
    c = lax.axis_index("cluster")
    i = lax.axis_index("view")
    s = 1 - 2 * lax.rem(i, 2)

    def at(k):
        return lax.rem(i + k * s + 64, 32)

    sib, va, vb, vf, vg, ve = at(1), at(-1), at(3), at(2), at(-2), at(-3)
    zp, zm = lax.rem(c + 1, 8), lax.rem(c + 7, 8)

    peers = [(c, sib), (c, va), (c, vb), (c, vf), (c, vg), (zp, i), (zm, i)]
    x = lax.rem(i // 2, 4)
    roles = []
    for k, (pc, pi) in enumerate(peers):
        if k < 5:
            px = lax.rem(pi // 2, 4)
            roles.append(((x == 0) & (px == 3), (x == 3) & (px == 0)))
        else:
            roles.append((pc > c, pc < c))
    opens = [r[0] for r in roles]

    if COMM:
        bar = pltpu.get_barrier_semaphore()
        count = jnp.int32(0)
        for (pc, pi), (mine, later) in zip(peers, roles):
            @pl.when(jnp.logical_not(later))
            def _():
                pl.semaphore_signal(bar, inc=1, device_id=(pc, pi), device_id_type=MESH)
            count = count + jnp.where(mine, 0, 1).astype(jnp.int32)

    def load(src, dst, sem):
        cp = pltpu.make_async_copy(src, dst, sem)
        cp.start()
        return cp

    l_raw = load(lat_hbm, raw, lsem.at[0])
    l_gain = load(gain_hbm, gain, lsem.at[1])
    l_kv = []
    for p in range(NP):
        cols = pl.ds(p * PAIR, PAIR)
        l_kv.append((load(wk_hbm.at[:, cols], wkv.at[p, :, pl.ds(0, PAIR)], wsem.at[2 * p]),
                     load(wv_hbm.at[:, cols], wkv.at[p, :, pl.ds(PAIR, PAIR)], wsem.at[2 * p + 1])))
    l_q = load(wq_hbm, wq, lsem.at[2])
    l_pl = load(pl_hbm, plist, lsem.at[3])
    l_o = load(wo_hbm, wo, lsem.at[4])

    if COMM:
        @pl.when(count > 0)
        def _():
            pl.semaphore_wait(bar, count)
        for slot, k in ((0, 1), (1, 2), (2, 4), (3, 6), (4, 5)):
            @pl.when(roles[k][1])
            def _():
                pl.semaphore_signal(ack.at[slot], inc=1, device_id=peers[k], device_id_type=MESH)

    l_raw.wait()
    l_gain.wait()
    flat = raw[...].astype(F32)
    mean = jnp.sum(flat, axis=1, keepdims=True) * (1.0 / D)
    cen = flat - mean
    var = jnp.sum(cen * cen, axis=1, keepdims=True) * (1.0 / D)
    own[...] = (cen * lax.rsqrt(var + 1e-05) * gain[...].reshape(1, D)).astype(BF)

    class Nop:
        def start(self): pass
        def wait(self): pass
        def wait_send(self): pass
        def wait_recv(self): pass

    names = "aabzZffssssss"

    def remote(src, dst, k, dev):
        if names[k] not in SENDS:
            return Nop()
        return pltpu.make_async_remote_copy(src_ref=src, dst_ref=dst, send_sem=ssem.at[k], recv_sem=rsem.at[k],
                                            device_id=dev, device_id_type=MESH)

    half = TOK // 2
    r_a = [remote(own.at[pl.ds(h * half, half)], xb.at[pl.ds(h * half, half)], h, (c, va)) for h in (0, 1)]
    r_b = remote(own, xb.at[pl.ds(TOK, TOK)], 2, (c, vb))
    r_zp = remote(own, xz.at[pl.ds(TOK, TOK)], 3, (zp, i))
    r_zm = remote(own, xz.at[pl.ds(0, TOK)], 4, (zm, i))
    r_f = [remote(xb.at[pl.ds(h * half, half)], xe.at[pl.ds(h * half, half)], 5 + h, (c, vf)) for h in (0, 1)]

    def share(k, g, row, gd, rowd):
        return (remote(kbuf.at[g, :, pl.ds(row, TOK), :], kbuf.at[gd, :, pl.ds(rowd, TOK), :], 7 + 2 * k, (c, sib)),
                remote(vt.at[g, :, pl.ds(0, PAIR), pl.ds(row, TOK)], vt.at[gd, :, pl.ds(0, PAIR), pl.ds(rowd, TOK)], 8 + 2 * k, (c, sib)))

    sh_own = share(0, GA, 0, GA, TOK)
    sh_a = share(1, GB, 0, GD, 0)
    sh_b = share(2, GB, TOK, GD, TOK)

    def early(copies, k):
        @pl.when(jnp.logical_not(opens[k]))
        def _():
            for cp in copies:
                cp.start()

    def late(copies, k, slot):
        @pl.when(opens[k])
        def _():
            pl.semaphore_wait(ack.at[slot], 1)
            for cp in copies:
                cp.start()

    if COMM:
        early(r_a, 1)
        early([r_zp], 5)
        early([r_zm], 6)
        if not LATEB:
            early([r_b], 2)

    vt[:, :, PAIR:PAIR + 16, :] = jnp.ones((5, NP, 16, 256), BF)
    qt[...] = jnp.zeros((NP, PAIR, 256), BF)

    def project(g, x, row, rows, p):
        kv = dot(x[...], wkv[p])
        kbuf[g, p, row:row + rows, :] = kv[:, :PAIR].astype(BF)
        vt[g, p, 0:PAIR, row:row + rows] = kv[:, PAIR:].astype(BF).T

    def scores(g, p, n):
        return dot(kbuf[g, p, 0:n, :], qt[p])

    def finish(st, g, p, bs, first):
        n = st.shape[0]
        mo = None if first else mx[p]
        tops = [jnp.max(st[k * TOK:(k + 1) * TOK], axis=0, keepdims=True) + b for k, b in enumerate(bs)]
        if not first:
            tops.append(mo)
        m = functools.reduce(jnp.maximum, tops)
        pr = [jnp.exp(st[k * TOK:(k + 1) * TOK] - (m - b)).astype(BF) for k, b in enumerate(bs)]
        pt = jnp.concatenate(pr, axis=0) if len(pr) > 1 else pr[0]
        o = dot(vt[g, p, :, 0:n], pt)
        mx[p] = m
        if first:
            tot[p] = o[PAIR:PAIR + 1]
            acc[p, 0:64, :] = o[0:64, 0:TOK]
            acc[p, 64:128, :] = o[64:128, TOK:]
        else:
            al = jnp.exp(mo - m)
            tot[p] = tot[p] * al + o[PAIR:PAIR + 1]
            acc[p, 0:64, :] = acc[p, 0:64, :] * al[:, 0:TOK] + o[0:64, 0:TOK]
            acc[p, 64:128, :] = acc[p, 64:128, :] * al[:, TOK:] + o[64:128, TOK:]

    def attend(tag, g, bs, first=False, beside=None, ahead=DEP):
        if tag in SKIP:
            return
        n = TOK * len(bs)
        held = [scores(g, p, n) for p in range(ahead)]
        for p in range(NP):
            if p + ahead < NP:
                held.append(scores(g, p + ahead, n))
            if beside:
                beside(p)
            finish(held[p], g, p, bs, first)

    def loop(body, tag=""):
        if tag and tag in SKIP:
            return
        if UN == 8:
            for p in range(NP):
                body(p)
        else:
            lax.fori_loop(0, NP, lambda p, _: (body(p), 0)[1], 0, unroll=UN)

    for p in range(NP):
        l_kv[p][0].wait()
        l_kv[p][1].wait()
    loop(lambda p: project(GA, own, 0, TOK, p), "a")
    if COMM:
        late(r_a, 1, 0)
        if LATEB:
            early([r_b], 2)
        late([r_b], 2, 1)
        for cp in sh_own:
            cp.start()
    l_q.wait()

    def queries(p):
        q = (dot(own[...], wq[:, pl.ds(pl.multiple_of(p * PAIR, PAIR), PAIR)]).astype(BF).astype(F32) * 0.125).T.astype(BF)
        qt[p, 0:64, 0:TOK] = q[0:64]
        qt[p, 64:128, TOK:] = q[64:128]
    loop(queries, "q")
    if COMM:
        late([r_zp], 5, 3)

    l_pl.wait()
    me = c * 32 + i
    first, second = plist[0:1, :], plist[1:2, :]
    ids = [c * 32 + sib, c * 32 + va, zp * 32 + i, c * 32 + vb, zm * 32 + i, c * 32 + vf, c * 32 + vg, c * 32 + ve]
    for k, other in enumerate(ids):
        match = ((first == me) & (second == other)) | ((first == other) & (second == me))
        found = jnp.max(jnp.where(match, 1.0, 0.0), axis=1, keepdims=True)
        bias[k] = jnp.broadcast_to(jnp.where(found > 0.5, 0.0, NONE), (1, 256))
    bz = jnp.zeros((1, 256), F32)

    def recv(copies):
        if COMM:
            for cp in copies:
                cp.wait_recv()

    def norm(p):
        inv = 1.0 / tot[p]
        top = acc[p, 0:64, :] * inv[:, 0:TOK]
        low = acc[p, 64:128, :] * inv[:, TOK:]
        mg[:, pl.ds(pl.multiple_of(p * PAIR, PAIR), PAIR)] = jnp.concatenate([top, low], axis=0).T.astype(BF)
    recv(sh_own)
    attend("A", GA, [bz, bias[0]], True)
    if COMM:
        @pl.when(opens[3])
        def _():
            pl.semaphore_wait(ack.at[2], 1)
        for h in (0, 1):
            r_a[h].wait_recv()
            r_f[h].start()
    loop(lambda p: project(GB, xb.at[pl.ds(0, TOK)], 0, TOK, p), "a")
    if COMM:
        for cp in sh_a:
            cp.start()
        late([r_zm], 6, 4)
    recv([r_b])
    loop(lambda p: project(GB, xb.at[pl.ds(TOK, TOK)], TOK, TOK, p), "b")
    if COMM:
        for cp in sh_b:
            cp.start()
    attend("B", GB, [bias[1], bias[3]])
    recv(sh_a + sh_b)
    recv([r_zm, r_zp])
    attend("D", GD, [bias[5], bias[6]], False, lambda p: project(GZ, xz, 0, 256, p))
    attend("Z", GZ, [bias[2], bias[4]])
    recv(r_f)
    loop(lambda p: project(GE, xe, 0, TOK, p), "e")
    attend("E", GE, [bias[7]], ahead=DEPE)
    loop(norm, "n")
    if XDOT:
        outv[...] = mg[...]
        l_o.wait()
    else:
        l_o.wait()
        for n in range(0 if 'o' in SKIP else 4):
            outv[:, n * 256:(n + 1) * 256] = dot(mg[...], wo[:, n * 256:(n + 1) * 256]).astype(BF)
    cp = pltpu.make_async_copy(outv, out_hbm, osem)
    cp.start()
    if COMM:
        for r in list(r_a) + [r_b, r_zp, r_zm] + list(r_f) + list(sh_own) + list(sh_a) + list(sh_b):
            r.wait_send()
    cp.wait()


def finish_copy(src, dst, sem):
    parts = [pltpu.make_async_copy(src.at[pl.ds(k * 32, 32)], dst.at[pl.ds(k * 32, 32)], sem.at[k]) for k in range(4)]
    for part in parts:
        part.start()
    for part in parts:
        part.wait()


def body(latents, gain, w_query, w_key, w_value, w_out, pair_list):
    V = pltpu.VMEM
    any_ = pl.BlockSpec(memory_space=pl.ANY)
    out = pl.pallas_call(
        kernel,
        out_shape=jax.ShapeDtypeStruct((TOK, D), BF),
        in_specs=[any_] * 7,
        out_specs=any_,
        scratch_shapes=[
            V((TOK, D), BF), V((D,), F32), V((D, D), BF), V((NP, D, 256), BF), V((D, D), BF), V((3, 512), jnp.int32),
            V((TOK, D), BF), V((256, D), BF), V((256, D), BF), V((TOK, D), BF),
            V((5, NP, 256, PAIR), BF), V((5, NP, PAIR + 16, 256), BF), V((NP, PAIR, 256), BF),
            V((NP, PAIR, TOK), F32), V((NP, 1, 256), F32), V((NP, 1, 256), F32), V((8, 1, 256), F32),
            V((TOK, D), BF), V((TOK, D), BF),
            pltpu.SemaphoreType.DMA((5,)), pltpu.SemaphoreType.DMA((16,)), pltpu.SemaphoreType.DMA,
            pltpu.SemaphoreType.DMA((13,)), pltpu.SemaphoreType.DMA((13,)), pltpu.SemaphoreType.REGULAR((5,)),
        ],
        compiler_params=pltpu.CompilerParams(collective_id=0 if COMM else None, has_side_effects=True, vmem_limit_bytes=VL),
    )(latents.reshape(TOK, D), gain, w_query, w_key, w_value, w_out, pair_list.T)
    if COPYK:
        out = pl.pallas_call(
            finish_copy, out_shape=jax.ShapeDtypeStruct((TOK, D), BF), in_specs=[any_], out_specs=any_,
            scratch_shapes=[pltpu.SemaphoreType.DMA((4,))])(out)
    if XDOT:
        out = jnp.dot(out, w_out, preferred_element_type=F32).astype(BF)
    return out.reshape(1, 1, TOK, D)


def solution(mesh):
    in_specs = (P("cluster", "view", None, None), P(), P(), P(), P(), P(), P())
    out_specs = P("cluster", "view", None, None)
    return jax.shard_map(body, mesh=mesh, in_specs=in_specs, out_specs=out_specs, check_vma=False)
```

profile of v0, /device:TPU:31, one launch (start us, length us, event | category | flops | bytes accessed | tf_op | source)
XLA Modules:
  0.0 23.9 jit_solution(8671726013230653648)
XLA Ops:
  0.0 22.3 %shard_map.73 = bf16[128,1024]{1,0:T(8,128)(2,1)} custom-call(bf16[128,1024]{1,0:T(8,128)(2,1)} %bitcast.4, f32[1024]{0:T(1024)} %gain_hbm.1, bf16[1024,1024]{1,0:T(8,128)(2,1)} %wq_hbm.1, bf16[1024,1024]{1,0:T(8,128)(2,1)} %wk_hbm.1, bf16[1024,1024]{1,0:T(8,128)(2,1)} %wv_hbm.1, bf16[1024,1024]{1,0:T(8,128)(2,1)} %wo_hbm.1, s32[3,512]{1,0:T(4,128)} %bitcast.5), custom_call_target="tpu_custom_call" | custom-call | tf_op jit(solution)/shard_map/pallas_call | solution.py:294
  22.3 1.7 %copy.9 = bf16[1,1,128,1024]{3,2,1,0:T(8,128)(2,1)} copy(bf16[1,1,128,1024]{3,2,1,0:T(8,128)(2,1)} %bitcast.3) | data formatting | bytes 524288
where the time goes:
time: 24.1 us; the launch traced here: 23.9 us
  Pallas kernels  22.3 us (93%)
  local copies, waits for them, and re-layouts  1.67 us (7%)
    pallas_call x1, Pallas kernels, body(): pl.pallas_call(kernel, out_shape=jax.ShapeDtypeStruct((TOK, D), BF), in_s...  22.3 us
    unnamed x1, local copies, waits for them, and re-layouts  1.67 us

commit v1 on v0

--- a/solution.py
+++ b/solution.py
@@ -18,6 +18,9 @@
 DEP = 2
 DEPE = 2
 LATEB = True
+LATEZ = False
+ORDER = 1
+CH = 2
 COPYK = False
 XDOT = False
 VL = 62 * 2**20
@@ -100,7 +103,7 @@
         def wait_send(self): pass
         def wait_recv(self): pass
 
-    names = "aabzZffssssss"
+    names = "aabzZffssssssaaaaffff"
 
     def remote(src, dst, k, dev):
         if names[k] not in SENDS:
@@ -108,12 +111,12 @@
         return pltpu.make_async_remote_copy(src_ref=src, dst_ref=dst, send_sem=ssem.at[k], recv_sem=rsem.at[k],
                                             device_id=dev, device_id_type=MESH)
 
-    half = TOK // 2
-    r_a = [remote(own.at[pl.ds(h * half, half)], xb.at[pl.ds(h * half, half)], h, (c, va)) for h in (0, 1)]
+    half = TOK // CH
+    r_a = [remote(own.at[pl.ds(h * half, half)], xb.at[pl.ds(h * half, half)], 13 + h, (c, va)) for h in range(CH)]
     r_b = remote(own, xb.at[pl.ds(TOK, TOK)], 2, (c, vb))
     r_zp = remote(own, xz.at[pl.ds(TOK, TOK)], 3, (zp, i))
     r_zm = remote(own, xz.at[pl.ds(0, TOK)], 4, (zm, i))
-    r_f = [remote(xb.at[pl.ds(h * half, half)], xe.at[pl.ds(h * half, half)], 5 + h, (c, vf)) for h in (0, 1)]
+    r_f = [remote(xb.at[pl.ds(h * half, half)], xe.at[pl.ds(h * half, half)], 17 + h, (c, vf)) for h in range(CH)]
 
     def share(k, g, row, gd, rowd):
         return (remote(kbuf.at[g, :, pl.ds(row, TOK), :], kbuf.at[gd, :, pl.ds(rowd, TOK), :], 7 + 2 * k, (c, sib)),
@@ -138,8 +141,9 @@
 
     if COMM:
         early(r_a, 1)
-        early([r_zp], 5)
-        early([r_zm], 6)
+        if not LATEZ:
+            early([r_zp], 5)
+            early([r_zm], 6)
         if not LATEB:
             early([r_b], 2)
 
@@ -204,6 +208,9 @@
         late(r_a, 1, 0)
         if LATEB:
             early([r_b], 2)
+        if LATEZ:
+            early([r_zp], 5)
+            early([r_zm], 6)
         late([r_b], 2, 1)
         for cp in sh_own:
             cp.start()
@@ -243,26 +250,50 @@
         @pl.when(opens[3])
         def _():
             pl.semaphore_wait(ack.at[2], 1)
-        for h in (0, 1):
+        for h in range(CH):
             r_a[h].wait_recv()
             r_f[h].start()
+        late([r_zm], 6, 4)
     loop(lambda p: project(GB, xb.at[pl.ds(0, TOK)], 0, TOK, p), "a")
     if COMM:
         for cp in sh_a:
             cp.start()
-        late([r_zm], 6, 4)
     recv([r_b])
     loop(lambda p: project(GB, xb.at[pl.ds(TOK, TOK)], TOK, TOK, p), "b")
     if COMM:
         for cp in sh_b:
             cp.start()
-    attend("B", GB, [bias[1], bias[3]])
-    recv(sh_a + sh_b)
-    recv([r_zm, r_zp])
-    attend("D", GD, [bias[5], bias[6]], False, lambda p: project(GZ, xz, 0, 256, p))
-    attend("Z", GZ, [bias[2], bias[4]])
-    recv(r_f)
-    loop(lambda p: project(GE, xe, 0, TOK, p), "e")
+    def proj_z(p):
+        project(GZ, xz, 0, 256, p)
+
+    def proj_e(p):
+        project(GE, xe, 0, TOK, p)
+
+    if ORDER in (1, 2):
+        recv([r_zm, r_zp])
+        attend("B", GB, [bias[1], bias[3]], False, proj_z)
+        attend("Z", GZ, [bias[2], bias[4]])
+    if ORDER == 3:
+        attend("B", GB, [bias[1], bias[3]])
+        recv([r_zm, r_zp])
+        loop(proj_z, "Z")
+        attend("Z", GZ, [bias[2], bias[4]])
+    if ORDER == 4:
+        attend("B", GB, [bias[1], bias[3]])
+        recv(sh_a + sh_b)
+        recv([r_zm, r_zp])
+        attend("D", GD, [bias[5], bias[6]], False, proj_z)
+        recv(r_f)
+        attend("Z", GZ, [bias[2], bias[4]], False, proj_e)
+    if ORDER in (1, 3):
+        recv(sh_a + sh_b)
+        recv(r_f)
+        attend("D", GD, [bias[5], bias[6]], False, proj_e)
+    if ORDER == 2:
+        recv(sh_a + sh_b)
+        attend("D", GD, [bias[5], bias[6]])
+        recv(r_f)
+        loop(proj_e, "e")
     attend("E", GE, [bias[7]], ahead=DEPE)
     loop(norm, "n")
     if XDOT:
@@ -303,7 +334,7 @@
             V((NP, PAIR, TOK), F32), V((NP, 1, 256), F32), V((NP, 1, 256), F32), V((8, 1, 256), F32),
             V((TOK, D), BF), V((TOK, D), BF),
             pltpu.SemaphoreType.DMA((5,)), pltpu.SemaphoreType.DMA((16,)), pltpu.SemaphoreType.DMA,
-            pltpu.SemaphoreType.DMA((13,)), pltpu.SemaphoreType.DMA((13,)), pltpu.SemaphoreType.REGULAR((5,)),
+            pltpu.SemaphoreType.DMA((21,)), pltpu.SemaphoreType.DMA((21,)), pltpu.SemaphoreType.REGULAR((5,)),
         ],
         compiler_params=pltpu.CompilerParams(collective_id=0 if COMM else None, has_side_effects=True, vmem_limit_bytes=VL),
     )(latents.reshape(TOK, D), gain, w_query, w_key, w_value, w_out, pair_list.T)

time: 24.1 us -> 23.5 us (0.975)
  Pallas kernels: 22.3 us -> 21.7 us
    pallas_call x1, Pallas kernels: 22.3 us -> 21.7 us  [body(): pl.pallas_call(kernel, out_shape=jax.ShapeDtypeStruct((TOK, D), BF), in_s...]
where the time goes in v1:
time: 23.5 us; the launch traced here: 23.4 us
  Pallas kernels  21.7 us (92%)
  local copies, waits for them, and re-layouts  1.67 us (7%)
    pallas_call x1, Pallas kernels, body(): pl.pallas_call(kernel, out_shape=jax.ShapeDtypeStruct((TOK, D), BF), in_s...  21.7 us
    unnamed x1, local copies, waits for them, and re-layouts  1.67 us

profile of v1, /device:TPU:31, one launch (start us, length us, event | category | flops | bytes accessed | tf_op | source)
XLA Modules:
  0.0 23.4 jit_solution(11135865182901061091)
XLA Ops:
  0.0 21.7 %shard_map.73 = bf16[128,1024]{1,0:T(8,128)(2,1)} custom-call(bf16[128,1024]{1,0:T(8,128)(2,1)} %bitcast.4, f32[1024]{0:T(1024)} %gain_hbm.1, bf16[1024,1024]{1,0:T(8,128)(2,1)} %wq_hbm.1, bf16[1024,1024]{1,0:T(8,128)(2,1)} %wk_hbm.1, bf16[1024,1024]{1,0:T(8,128)(2,1)} %wv_hbm.1, bf16[1024,1024]{1,0:T(8,128)(2,1)} %wo_hbm.1, s32[3,512]{1,0:T(4,128)} %bitcast.5), custom_call_target="tpu_custom_call" | custom-call | tf_op jit(solution)/shard_map/pallas_call | solution.py:325
  21.7 1.7 %copy.9 = bf16[1,1,128,1024]{3,2,1,0:T(8,128)(2,1)} copy(bf16[1,1,128,1024]{3,2,1,0:T(8,128)(2,1)} %bitcast.3) | data formatting | bytes 524288

commit v2 on v1

--- a/solution.py
+++ b/solution.py
@@ -15,7 +15,7 @@
 COMM = True
 SKIP = ""
 SENDS = "abzZfs"
-DEP = 2
+DEP = 3
 DEPE = 2
 LATEB = True
 LATEZ = False
@@ -205,6 +205,8 @@
         l_kv[p][1].wait()
     loop(lambda p: project(GA, own, 0, TOK, p), "a")
     if COMM:
+        for cp in sh_own:
+            cp.start()
         late(r_a, 1, 0)
         if LATEB:
             early([r_b], 2)
@@ -212,8 +214,6 @@
             early([r_zp], 5)
             early([r_zm], 6)
         late([r_b], 2, 1)
-        for cp in sh_own:
-            cp.start()
     l_q.wait()
 
     def queries(p):
@@ -296,19 +296,18 @@
         loop(proj_e, "e")
     attend("E", GE, [bias[7]], ahead=DEPE)
     loop(norm, "n")
-    if XDOT:
-        outv[...] = mg[...]
-        l_o.wait()
-    else:
-        l_o.wait()
-        for n in range(0 if 'o' in SKIP else 4):
-            outv[:, n * 256:(n + 1) * 256] = dot(mg[...], wo[:, n * 256:(n + 1) * 256]).astype(BF)
-    cp = pltpu.make_async_copy(outv, out_hbm, osem)
-    cp.start()
+    l_o.wait()
+    stores = []
+    for n in range(4):
+        cols = pl.ds(n * 256, 256)
+        outv[:, cols] = dot(mg[...], wo[:, cols]).astype(BF)
+        stores.append(pltpu.make_async_copy(outv.at[:, cols], out_hbm.at[:, cols], osem.at[n]))
+        stores[-1].start()
     if COMM:
         for r in list(r_a) + [r_b, r_zp, r_zm] + list(r_f) + list(sh_own) + list(sh_a) + list(sh_b):
             r.wait_send()
-    cp.wait()
+    for cp in stores:
+        cp.wait()
 
 
 def finish_copy(src, dst, sem):
@@ -333,7 +332,7 @@
             V((5, NP, 256, PAIR), BF), V((5, NP, PAIR + 16, 256), BF), V((NP, PAIR, 256), BF),
             V((NP, PAIR, TOK), F32), V((NP, 1, 256), F32), V((NP, 1, 256), F32), V((8, 1, 256), F32),
             V((TOK, D), BF), V((TOK, D), BF),
-            pltpu.SemaphoreType.DMA((5,)), pltpu.SemaphoreType.DMA((16,)), pltpu.SemaphoreType.DMA,
+            pltpu.SemaphoreType.DMA((5,)), pltpu.SemaphoreType.DMA((16,)), pltpu.SemaphoreType.DMA((4,)),
             pltpu.SemaphoreType.DMA((21,)), pltpu.SemaphoreType.DMA((21,)), pltpu.SemaphoreType.REGULAR((5,)),
         ],
         compiler_params=pltpu.CompilerParams(collective_id=0 if COMM else None, has_side_effects=True, vmem_limit_bytes=VL),

time: 23.5 us -> 23.4 us (level)
  no operation moved by 1% of the time
where the time goes in v2:
time: 23.4 us; the launch traced here: 23.3 us
  Pallas kernels  21.6 us (92%)
  local copies, waits for them, and re-layouts  1.67 us (7%)
    pallas_call x1, Pallas kernels, body(): pl.pallas_call(kernel, out_shape=jax.ShapeDtypeStruct((TOK, D), BF), in_s...  21.6 us
    unnamed x1, local copies, waits for them, and re-layouts  1.67 us

profile of v2, /device:TPU:31, one launch (start us, length us, event | category | flops | bytes accessed | tf_op | source)
XLA Modules:
  0.0 23.3 jit_solution(17491555227363575632)
XLA Ops:
  0.0 21.6 %shard_map.73 = bf16[128,1024]{1,0:T(8,128)(2,1)} custom-call(bf16[128,1024]{1,0:T(8,128)(2,1)} %bitcast.4, f32[1024]{0:T(1024)} %gain_hbm.1, bf16[1024,1024]{1,0:T(8,128)(2,1)} %wq_hbm.1, bf16[1024,1024]{1,0:T(8,128)(2,1)} %wk_hbm.1, bf16[1024,1024]{1,0:T(8,128)(2,1)} %wv_hbm.1, bf16[1024,1024]{1,0:T(8,128)(2,1)} %wo_hbm.1, s32[3,512]{1,0:T(4,128)} %bitcast.5), custom_call_target="tpu_custom_call" | custom-call | tf_op jit(solution)/shard_map/pallas_call | solution.py:324
  21.7 1.7 %copy.9 = bf16[1,1,128,1024]{3,2,1,0:T(8,128)(2,1)} copy(bf16[1,1,128,1024]{3,2,1,0:T(8,128)(2,1)} %bitcast.3) | data formatting | bytes 524288
